TPU v7x, 128 devices: a whole 4x4x4 slice. The times are simulated.
128 devices in a mesh: dp: 32 (over y, x, z_hi), tensor: 4 (over z_lo, core).
Axes of the slice: x: 4, y: 4, z: 4 (z_hi: 2, z_lo: 2; z = z_hi * 2 + z_lo), core: 2. Of those that a mesh axis runs over, the one named last changes fastest.
Arguments:
- tokens: bfloat16 [16384, 4096], P('dp', 'tensor'), may hold values from -6 to 6
- out_cot: bfloat16 [16384, 4096], P('dp', 'tensor'), may hold values from -6 to 6
- kept_sections: int32 [64, 2], P('tensor'), may hold values from 0 to 3, as said below
- w_in: bfloat16 [64, 3, 256, 256], P('tensor', None, 'dp'), may hold values from -0.21875 to 0.21875
- w_out: bfloat16 [64, 3, 256, 256], P('tensor', None, 'dp'), may hold values from -0.109375 to 0.109375
Outputs:
- mixed: bfloat16 [16384, 4096], P('dp', 'tensor')
- tokens_grad: bfloat16 [16384, 4096], P('dp', 'tensor')
- w_in_grad: float32 [64, 3, 256, 256], P('tensor', None, 'dp')
- w_out_grad: float32 [64, 3, 256, 256], P('tensor', None, 'dp')
Inputs may be any that keep to these rules, and one draw needn't show every extreme that they name: `kept_sections`: each row names 2 different sections.
All inputs are finite; a program needn't handle non-finite values.
Results may differ from a plain program's by a relative error of at most 0.018.
Values may be sent and summed in bfloat16 or wider, within the bound.
A program may use at most 192 MiB of HBM per device.

v0:
```python
import jax
import jax.numpy as jnp
import numpy as np
from jax import lax
from jax.sharding import PartitionSpec as P


def swapped(value, axis, distance):
    return lax.ppermute(value, axis, [(i, i ^ 1 << distance) for i in range(lax.axis_size(axis))])


def gelu_slope(pre):
    cdf = 0.5 * (1.0 + lax.erf(pre * 0.7071067811865476))
    return cdf + pre * jnp.exp(-0.5 * pre * pre) * 0.3989422804014327


def per_device(tokens, out_cot, kept_sections, w_in, w_out):
    token_rows = tokens.shape[0]
    width = tokens.shape[1]
    block_size = w_in.shape[3]
    hidden_local = w_in.shape[0]
    slot_count = w_in.shape[1]
    group_count = width // block_size
    per_group = hidden_local // group_count
    kinds_total = 5
    scale = float(token_rows * lax.axis_size("dp")) ** (-0.5)
    bit_total = lax.axis_size("tensor").bit_length() - 1
    flip_one = np.arange(group_count) ^ 1
    flip_two = np.arange(group_count) ^ 2
    full_in, full_out = (
        lax.all_gather(w_in, "dp", axis=2, tiled=True),
        lax.all_gather(w_out, "dp", axis=2, tiled=True),
    )
    near_tokens = []
    near_cot = []
    for bit_index in range(bit_total):
        got_tokens, got_cot = swapped((tokens, out_cot), "tensor", bit_index)
        near_tokens.append(got_tokens)
        near_cot.append(got_cot)

    def candidates(local, near):
        own_blocks = local.reshape(token_rows, group_count, block_size)
        stacked = [own_blocks, own_blocks[:, flip_one], own_blocks[:, flip_two]]
        stacked = stacked + [piece.reshape(token_rows, group_count, block_size) for piece in near]
        return jnp.stack(stacked, axis=2)

    slot_kind = jnp.concatenate(
        [jnp.zeros((hidden_local, 1), jnp.int32), kept_sections + 1], axis=1
    )
    group_index = jnp.broadcast_to(
        (jnp.arange(hidden_local, dtype=jnp.int32) // per_group)[:, None], slot_kind.shape
    )
    kind_mask = (
        slot_kind[:, :, None] == jnp.arange(kinds_total, dtype=jnp.int32)[None, None, :]
    ).astype(jnp.float32)
    kind_mask = kind_mask.reshape(group_count, per_group, slot_count, kinds_total)

    def deliver(terms):
        grouped = terms.reshape(token_rows, group_count, per_group, slot_count, block_size)
        by_kind = jnp.einsum(
            "tgjso,gjsk->tkgo", grouped, kind_mask, precision=lax.Precision.HIGHEST
        )
        local = by_kind[:, 0] + by_kind[:, 1][:, flip_one] + by_kind[:, 2][:, flip_two]
        return (local, [by_kind[:, 3], by_kind[:, 4]])

    picked = candidates(tokens, near_tokens)[:, group_index, slot_kind]
    pre = jnp.einsum("thsi,hsio->tho", picked, full_in, preferred_element_type=jnp.float32)
    act = jax.nn.gelu(pre, approximate=False).astype(jnp.bfloat16)
    terms = jnp.einsum("thi,hsio->thso", act, full_out, preferred_element_type=jnp.float32)
    mixed_local, mixed_far = deliver(terms)
    dpicked = candidates(out_cot, near_cot)[:, group_index, slot_kind]
    out_term = (
        jnp.einsum("thi,thso->hsio", act, dpicked, preferred_element_type=jnp.float32) * scale
    )
    act_grad = jnp.einsum("thso,hsio->thi", dpicked, full_out, preferred_element_type=jnp.float32)
    pre_grad = (act_grad * gelu_slope(pre)).astype(jnp.bfloat16)
    in_term = (
        jnp.einsum("thsi,tho->hsio", picked, pre_grad, preferred_element_type=jnp.float32) * scale
    )
    back = jnp.einsum("tho,hsio->thsi", pre_grad, full_in, preferred_element_type=jnp.float32)
    grad_local, grad_far = deliver(back)
    w_in_grad, w_out_grad = (
        lax.psum_scatter(
            in_term.astype(jnp.bfloat16), "dp", scatter_dimension=2, tiled=True
        ).astype(jnp.float32),
        lax.psum_scatter(
            out_term.astype(jnp.bfloat16), "dp", scatter_dimension=2, tiled=True
        ).astype(jnp.float32),
    )
    for bit_index in range(bit_total):
        recv_mixed, recv_grad = (
            swapped(mixed_far[bit_index].astype(jnp.bfloat16), "tensor", bit_index).astype(
                jnp.float32
            ),
            swapped(grad_far[bit_index].astype(jnp.bfloat16), "tensor", bit_index).astype(
                jnp.float32
            ),
        )
        mixed_local = mixed_local + recv_mixed
        grad_local = grad_local + recv_grad
    mixed = mixed_local.reshape(token_rows, width).astype(jnp.bfloat16)
    tokens_grad = grad_local.reshape(token_rows, width).astype(jnp.bfloat16)
    return (mixed, tokens_grad, w_in_grad, w_out_grad)


def solution(mesh):
    in_specs = (
        P("dp", "tensor"),
        P("dp", "tensor"),
        P("tensor", None),
        P("tensor", None, "dp", None),
        P("tensor", None, "dp", None),
    )
    out_specs = (
        P("dp", "tensor"),
        P("dp", "tensor"),
        P("tensor", None, "dp", None),
        P("tensor", None, "dp", None),
    )
    return jax.shard_map(
        per_device, mesh=mesh, in_specs=in_specs, out_specs=out_specs, check_vma=False
    )
```

profile of v0, /device:TPU:0, one launch (start us, length us, event | category | flops | bytes accessed | tf_op | source)
XLA Modules:
  0.0 770.6 jit_solution(17516045636260956200)
XLA Ops:
  8.7 2.3 copy.101
  11.0 2.0 collective-permute-start.5
  21.0 1.6 gather_fusion.5
  23.4 2.3 copy.107
  27.0 2.4 constant_dynamic-update-slice_fusion.2
  29.3 2.3 constant_dynamic-update-slice_fusion.5
  31.6 2.3 bitcast_dynamic-update-slice_fusion.3
  33.9 2.4 bitcast_dynamic-update-slice_fusion.2
  39.9 2.3 copy.108
  42.1 22.1 %collective-permute-done.1 = bf16[512,1024]{0,1:T(8,128)(2,1)} collective-permute-done((bf16[512,1024]{0,1:T(8,128)(2,1)S(1)}, bf16[512,1024]{0,1:T(8,128)(2,1)}, u32[]{:S(2)}, u32[]{:S(2)}) %collective-permute-start.1) | collective-permute-done | bytes 1048608 | tf_op jit(solution)/shard_map/ppermute | solution.py:9
  64.2 2.3 copy.93
  69.1 2.3 constant_dynamic-update-slice_fusion
  71.4 5.2 copy.95
  78.8 5.3 copy.110
  84.1 8.9 %gather_fusion.7 = bf16[48,512,256]{2,1,0:T(8,128)(2,1)} fusion(bf16[512,4,5,256]{3,0,2,1:T(8,128)(2,1)} %copy.110, s32[48]{0:T(128)S(1)} %reshape.129), kind=kCustom, calls=%fused_computation.7 | custom fusion | bytes 25166208 | tf_op jit(solution)/shard_map/gather | solution.py:71
  93.0 9.0 %gather_fusion.2 = bf16[48,512,256]{2,1,0:T(8,128)(2,1)} fusion(bf16[512,4,5,256]{3,0,2,1:T(8,128)(2,1)} %copy.95, s32[48]{0:T(128)S(1)} %reshape.129), kind=kCustom, calls=%fused_computation.2 | custom fusion | bytes 25166208 | tf_op jit(solution)/shard_map/gather | solution.py:66
  102.0 16.7 %copy.96 = bf16[16,3,512,256]{2,3,1,0:T(8,128)(2,1)} copy(bf16[16,3,512,256]{3,2,1,0:T(8,128)(2,1)} %bitcast.227) | data formatting | bytes 25165824 | tf_op jit(solution)/shard_map/gather | solution.py:66
  118.8 8.2 %all-gather.3.cloned.1.call-done = bf16[16,3,256,256]{3,2,1,0:T(8,128)(2,1)} async-done(((bf16[16,3,8,256]{3,2,1,0:T(8,128)(2,1)}), bf16[16,3,256,256]{3,2,1,0:T(8,128)(2,1)}) %all-gather.3.cloned.1.call-update) | async-done | bytes 6291472 | tf_op jit(solution)/shard_map/all_gather | solution.py:31
  127.0 24.5 %fusion.16 = (bf16[512,16,256]{2,0,1:T(8,128)(2,1)}, f32[16,512,256,1]{2,1,3,0:T(8,128)}) fusion(bf16[512,16,3,256]{3,0,2,1:T(8,128)(2,1)} %bitcast.228, bf16[16,3,256,256]{3,2,1,0:T(8,128)(2,1)} %all-gather.3.cloned.1.call-done), kind=kOutput, calls=%fused_computation.26 | convolution fusion | flops 3357540352 | bytes 31457280 | tf_op jit(solution)/shard_map/thsi,hsio->tho/dot_general | solution.py:67
  151.5 88.7 %all-gather.5.cloned.1.call-done = bf16[16,3,256,256]{3,2,1,0:T(8,128)(2,1)} async-done(((bf16[16,3,8,256]{3,2,1,0:T(8,128)(2,1)}), bf16[16,3,256,256]{3,2,1,0:T(8,128)(2,1)}) %all-gather.5.cloned.1.call-update) | async-done | bytes 6291472 | tf_op jit(solution)/shard_map/all_gather | solution.py:32
  240.2 13.1 %fusion.22 = bf16[512,16,256]{2,0,1:T(8,128)(2,1)} fusion(f32[16,512,256,1]{2,1,3,0:T(8,128)} %get-tuple-element.31, bf16[512,16,3,256]{3,0,2,1:T(8,128)(2,1)} %bitcast.225, bf16[16,3,256,256]{3,2,1,0:T(8,128)(2,1)} %all-gather.5.cloned.1.call-done), kind=kOutput, calls=%fused_computation.32 | convolution fusion | flops 3242196992 | bytes 31457280 | tf_op jit(solution)/shard_map/thso,hsio->thi/dot_general | solution.py:75
  253.3 11.9 %multiply_convert_fusion.1 = bf16[16,3,256,256]{3,2,1,0:T(8,128)(2,1)} fusion(bf16[512,16,256]{2,0,1:T(8,128)(2,1)} %fusion.22, bf16[16,3,512,256]{2,3,1,0:T(8,128)(2,1)} %copy.96), kind=kOutput, calls=%fused_computation.19 | convolution fusion | flops 3227516928 | bytes 23068672 | tf_op jit(solution)/shard_map/thsi,tho->hsio/dot_general | solution.py:78
  265.2 11.4 %copy.190 = bf16[16,3,256,256]{3,1,0,2:T(4,128)(2,1)} copy(bf16[16,3,256,256]{3,2,1,0:T(8,128)(2,1)} %multiply_convert_fusion.1) | data formatting | bytes 12582912
  276.6 14.7 %reshape.201 = bf16[256,12288]{1,0:T(8,128)(2,1)} reshape(bf16[256,16,3,256]{3,2,1,0:T(4,128)(2,1)} %bitcast.229) | data formatting | bytes 12582912
  291.6 17.1 %copy.111 = bf16[16,3,512,256]{2,3,1,0:T(8,128)(2,1)} copy(bf16[16,3,512,256]{3,2,1,0:T(8,128)(2,1)} %bitcast.226) | data formatting | bytes 25165824 | tf_op jit(solution)/shard_map/gather | solution.py:71
  308.7 12.0 %fusion.37 = bf16[16,3,256,256]{2,3,1,0:T(8,128)(2,1)} fusion(bf16[512,16,256]{2,0,1:T(8,128)(2,1)} %get-tuple-element.30, bf16[16,3,512,256]{2,3,1,0:T(8,128)(2,1)} %copy.111), kind=kOutput, calls=%fused_computation.57 | convolution fusion | flops 3227516928 | bytes 23068672 | tf_op jit(solution)/shard_map/thi,thso->hsio/dot_general | solution.py:73
  320.7 9.1 %copy.116 = bf16[16,3,256,256]{3,0,1,2:T(8,128)(2,1)} copy(bf16[16,3,256,256]{2,3,1,0:T(8,128)(2,1)} %fusion.37) | data formatting | bytes 12582912 | tf_op jit(solution)/shard_map/convert_element_type | solution.py:87
  329.8 16.1 %fusion.42 = f32[16,512,3,256]{3,1,2,0:T(8,128)} fusion(bf16[16,3,256,256]{3,2,1,0:T(8,128)(2,1)} %all-gather.3.cloned.1.call-done, bf16[512,16,256]{2,0,1:T(8,128)(2,1)} %fusion.22), kind=kOutput, calls=%fused_computation.62 | convolution fusion | flops 3221225472 | bytes 35651584 | tf_op jit(solution)/shard_map/tho,hsio->thsi/dot_general | solution.py:80
  345.9 50.4 %fusion.76 = (bf16[512,5,4,256]{3,1,0,2:T(8,128)(2,1)S(1)}, f32[512,5,4,256]{3,1,0,2:T(8,128)}) fusion(f32[512,4,4,3,256]{4,0,3,2,1:T(8,128)} %bitcast.223, pred[4,4,3,5,1]{3,1,2,4,0:T(4,128)(4,1)S(1)} %fusion.63.clone.2), kind=kOutput, calls=%fused_computation.118 | convolution fusion | flops 380108800 | bytes 40894704 | tf_op jit(solution)/shard_map/tgjso,gjsk->tkgo/dot_general | solution.py:60
  396.4 3.9 fusion.73
  403.2 10.2 %fusion.39 = f32[16,512,3,256]{3,1,2,0:T(8,128)} fusion(bf16[16,3,256,256]{3,2,1,0:T(8,128)(2,1)S(1)} %bitcast.231, bf16[512,16,256]{2,0,1:T(8,128)(2,1)S(1)} %copy-done.1), kind=kOutput, calls=%fused_computation.59 | convolution fusion | flops 3221225472 | bytes 35651584 | tf_op jit(solution)/shard_map/thi,hsio->thso/dot_general | solution.py:69
  413.4 50.1 %fusion.75 = (bf16[512,5,4,256]{3,1,0,2:T(8,128)(2,1)}, f32[512,5,4,256]{3,1,0,2:T(8,128)S(1)}) fusion(f32[512,4,4,3,256]{4,0,3,2,1:T(8,128)} %bitcast.224, pred[4,4,3,5,1]{3,1,2,4,0:T(4,128)(4,1)S(1)} %fusion.64.clone.4), kind=kOutput, calls=%fused_computation.117 | convolution fusion | flops 380108800 | bytes 40894704 | tf_op jit(solution)/shard_map/tgjso,gjsk->tkgo/dot_general | solution.py:60
  463.5 10.0 %fusion.74 = (bf16[512,1,4,256]{3,1,0,2:T(2,128)(2,1)S(1)}, bf16[512,1,4,256]{3,1,0,2:T(2,128)(2,1)S(1)}) fusion(bf16[512,5,4,256]{3,1,0,2:T(8,128)(2,1)} %get-tuple-element.32), kind=kLoop, calls=%fused_computation.116 | loop fusion | bytes 4194304 | tf_op jit(solution)/shard_map/slice | solution.py:64
  475.9 1.7 collective-permute-start.3
  477.8 22.4 %fusion.71 = (f32[512,1,4,256]{3,1,0,2:T(1,128)S(1)}, f32[512,1,4,256]{3,1,0,2:T(1,128)}, f32[512,1,4,256]{3,1,0,2:T(1,128)}) fusion(f32[512,5,4,256]{3,1,0,2:T(8,128)} %get-tuple-element.35), kind=kLoop, calls=%fused_computation.113 | loop fusion | bytes 12582912 | tf_op jit(solution)/shard_map/slice | solution.py:63
  500.2 6.5 fusion.72
  506.8 2.2 gather_fusion.8
  508.9 1.7 copy.191
  510.7 2.1 gather_fusion.9
  512.8 1.7 copy.194
  514.5 2.2 gather_fusion.3
  516.6 1.7 copy.193
  518.4 2.1 gather_fusion.4
  520.5 4.2 fusion.56
  526.1 2.3 copy.118
  528.3 3.4 fusion.61
  535.7 226.2 %reduce-scatter.5.cloned.1.call-done = bf16[16,3,8,256]{3,0,1,2:T(8,128)(2,1)} async-done(((bf16[16,3,256,256]{3,0,1,2:T(8,128)(2,1)}), bf16[16,3,8,256]{3,0,1,2:T(8,128)(2,1)}) %reduce-scatter.5.cloned.1.call-update) | async-done | bytes 196624 | tf_op jit(solution)/shard_map/reduce_scatter | solution.py:86
  761.9 1.7 copy.119
  (85 shorter events, 31.2 us)
Async XLA Ops:
  7.2 10.0 %copy-start.9 = (s32[4]{0:T(128)S(1)}, s32[4]{0:T(128)}, u32[]{:S(2)}) copy-start(s32[4]{0:T(128)} %constant.134) | copy-start | bytes 52
  7.2 10.0 %copy-start.10 = (s32[4]{0:T(128)S(1)}, s32[4]{0:T(128)}, u32[]{:S(2)}) copy-start(s32[4]{0:T(128)} %constant.133) | copy-start | bytes 52
  7.2 119.8 %all-gather.3.cloned.1.call-start = ((), (), s32[]{:S(2)}) async-start(), calls=%async_computation.2 | async-start | bytes 6488064 | tf_op jit(solution)/shard_map/all_gather | solution.py:31
  7.9 232.3 %all-gather.5.cloned.1.call-start = ((), (), s32[]{:S(2)}) async-start(), calls=%async_computation.3 | async-start | bytes 6488064 | tf_op jit(solution)/shard_map/all_gather | solution.py:32
  8.7 14.0 %copy-start.8 = (s32[16,2]{0,1:T(2,128)S(1)}, s32[16,2]{0,1:T(2,128)}, u32[]{:S(2)}) copy-start(s32[16,2]{0,1:T(2,128)} %param.17) | copy-start | bytes 388
  8.7 524.9 %reduce-scatter.7.cloned.1.call-start = ((), (), s32[]{:S(2)}) async-start(), calls=%async_computation.5 | async-start | bytes 6488064
  11.0 27.4 %collective-permute-start.5 = (bf16[512,1024]{0,1:T(8,128)(2,1)}, bf16[512,1024]{0,1:T(8,128)(2,1)}, u32[]{:S(2)}, u32[]{:S(2)}) collective-permute-start(bf16[512,1024]{0,1:T(8,128)(2,1)} %copy.101), channel_id=1, source_target_pairs={{0,2},{1,3},{2,0},{3,1},{4,6},{5,7},{6,4},{7,5},{8,10},{9,11},{10,... | collective-permute-start | bytes 3145736 | tf_op jit(solution)/shard_map/ppermute | solution.py:9
  13.0 26.9 %collective-permute-start.4 = (bf16[512,1024]{0,1:T(8,128)(2,1)}, bf16[512,1024]{0,1:T(8,128)(2,1)}, u32[]{:S(2)}, u32[]{:S(2)}) collective-permute-start(bf16[512,1024]{0,1:T(8,128)(2,1)} %copy.101), channel_id=1, source_target_pairs={{0,1},{1,0},{2,3},{3,2},{4,5},{5,4},{6,7},{7,6},{8,9},{9,8},{10,11... | collective-permute-start | bytes 3145736 | tf_op jit(solution)/shard_map/ppermute | solution.py:9
  14.5 49.7 %collective-permute-start.1 = (bf16[512,1024]{0,1:T(8,128)(2,1)S(1)}, bf16[512,1024]{0,1:T(8,128)(2,1)}, u32[]{:S(2)}, u32[]{:S(2)}) collective-permute-start(bf16[512,1024]{0,1:T(8,128)(2,1)S(1)} %copy.85), channel_id=1, source_target_pairs={{0,2},{1,3},{2,0},{3,1},{4,6},{5,7},{6,4},{7,5},{8,10},{9,11},{10,... | collective-permute-start | bytes 3145736 | tf_op jit(solution)/shard_map/ppermute | solution.py:9
  14.6 51.9 %collective-permute-start = (bf16[512,1024]{0,1:T(8,128)(2,1)S(1)}, bf16[512,1024]{0,1:T(8,128)(2,1)}, u32[]{:S(2)}, u32[]{:S(2)}) collective-permute-start(bf16[512,1024]{0,1:T(8,128)(2,1)S(1)} %copy.85), channel_id=1, source_target_pairs={{0,1},{1,0},{2,3},{3,2},{4,5},{5,4},{6,7},{7,6},{8,9},{9,8},{10,11... | collective-permute-start | bytes 3145736 | tf_op jit(solution)/shard_map/ppermute | solution.py:9
  17.2 14.4 %copy-start.4 = (s32[1024]{0:T(1024)}, s32[1024]{0:T(1024)S(1)}, u32[]{:S(2)}) copy-start(s32[1024]{0:T(1024)S(1)} %get-tuple-element.36) | copy-start | bytes 12292
  17.2 14.4 %copy-start.5 = (s32[1024]{0:T(1024)}, s32[1024]{0:T(1024)S(1)}, u32[]{:S(2)}) copy-start(s32[1024]{0:T(1024)S(1)} %get-tuple-element.37) | copy-start | bytes 12292
  22.6 0.5 copy-start.6
  27.0 9.3 %copy-start.2 = (bf16[4,512,256]{2,1,0:T(8,128)(2,1)S(1)}, bf16[4,512,256]{2,1,0:T(8,128)(2,1)}, u32[]{:S(2)}) copy-start(bf16[4,512,256]{2,1,0:T(8,128)(2,1)} %gather_fusion.5) | copy-start | bytes 3145732
  66.5 10.2 %copy-start.3 = (bf16[512,4,1,256]{3,0,1,2:T(8,128)(2,1)S(1)}, bf16[512,4,1,256]{3,0,1,2:T(8,128)(2,1)}, u32[]{:S(2)}) copy-start(bf16[512,4,1,256]{3,0,1,2:T(8,128)(2,1)} %copy.108) | copy-start | bytes 3145732
  276.6 14.7 %copy-start.7 = (s32[16,2]{0,1:T(2,128)S(1)}, s32[16,2]{0,1:T(2,128)}, u32[]{:S(2)}) copy-start(s32[16,2]{0,1:T(2,128)} %copy-done.6) | copy-start | bytes 388
  291.2 470.7 %reduce-scatter.5.cloned.1.call-start = ((), (), s32[]{:S(2)}) async-start(), calls=%async_computation.4 | async-start | bytes 6488064 | tf_op jit(solution)/shard_map/reduce_scatter | solution.py:86
  396.4 6.8 slice-start
  396.4 6.8 copy-start.1
  396.4 6.8 slice-start.1
  402.7 117.9 %collective-permute-start.7 = (bf16[512,4,256]{2,0,1:T(8,128)(2,1)}, bf16[512,4,256]{2,0,1:T(8,128)(2,1)}, u32[]{:S(2)}, u32[]{:S(2)}) collective-permute-start(bf16[512,4,256]{2,0,1:T(8,128)(2,1)} %bitcast.219), channel_id=1, source_target_pairs={{0,2},{1,3},{2,0},{3,1},{4,6},{5,7},{6,4},{7,5},{8,10},{9,11},{10,... | collective-permute-start | bytes 3145736 | tf_op jit(solution)/shard_map/ppermute | solution.py:9
  403.0 117.6 %collective-permute-start.6 = (bf16[512,4,256]{2,0,1:T(8,128)(2,1)}, bf16[512,4,256]{2,0,1:T(8,128)(2,1)}, u32[]{:S(2)}, u32[]{:S(2)}) collective-permute-start(bf16[512,4,256]{2,0,1:T(8,128)(2,1)} %bitcast.220), channel_id=1, source_target_pairs={{0,1},{1,0},{2,3},{3,2},{4,5},{5,4},{6,7},{7,6},{8,9},{9,8},{10,11... | collective-permute-start | bytes 3145736 | tf_op jit(solution)/shard_map/ppermute | solution.py:9
  475.9 52.5 %collective-permute-start.3 = (bf16[512,4,256]{2,0,1:T(8,128)(2,1)}, bf16[512,4,256]{2,0,1:T(8,128)(2,1)}, u32[]{:S(2)}, u32[]{:S(2)}) collective-permute-start(bf16[512,4,256]{2,0,1:T(8,128)(2,1)} %bitcast.221), channel_id=1, source_target_pairs={{0,2},{1,3},{2,0},{3,1},{4,6},{5,7},{6,4},{7,5},{8,10},{9,11},{10,... | collective-permute-start | bytes 3145736 | tf_op jit(solution)/shard_map/ppermute | solution.py:9
  477.6 50.8 %collective-permute-start.2 = (bf16[512,4,256]{2,0,1:T(8,128)(2,1)}, bf16[512,4,256]{2,0,1:T(8,128)(2,1)}, u32[]{:S(2)}, u32[]{:S(2)}) collective-permute-start(bf16[512,4,256]{2,0,1:T(8,128)(2,1)} %bitcast.222), channel_id=1, source_target_pairs={{0,1},{1,0},{2,3},{3,2},{4,5},{5,4},{6,7},{7,6},{8,9},{9,8},{10,11... | collective-permute-start | bytes 3145736 | tf_op jit(solution)/shard_map/ppermute | solution.py:9
  520.5 7.8 %copy-start = (f32[4,512,256]{2,1,0:T(8,128)S(1)}, f32[4,512,256]{2,1,0:T(8,128)}, u32[]{:S(2)}) copy-start(f32[4,512,256]{2,1,0:T(8,128)} %gather_fusion.3) | copy-start | bytes 6291460
Sparse Core Ops, SparseCore 0:
  10.8 116.1 all-gather.2
  129.7 110.4 all-gather.4
  291.4 236.0 reduce-scatter.6
  532.5 229.4 reduce-scatter.4
where the time goes:
time: 782 us; the launch traced here: 771 us
  waiting for transfers between devices  347 us (44%)
  local copies, waits for them, and re-layouts  207 us (26%)
  matrix products  188 us (24%)
  between operations  14.5 us (2%)
  other arithmetic  8.67 us (1%)
    reduce_scatter x1, waiting for transfers between devices, per_device(): lax.psum_scatter(out_term.astype(jnp.bfloat16), 'dp', scatter_dimension=2...  226 us
    dot_general x2, matrix products, deliver(): jnp.einsum('tgjso,gjsk->tkgo', grouped, kind_mask, precision=lax.Precisio...  101 us
    all_gather x1, waiting for transfers between devices, per_device(): lax.all_gather(w_out, 'dp', axis=2, tiled=True)  88.7 us
    unnamed x50, local copies, waits for them, and re-layouts  60.5 us
    slice x2, local copies, waits for them, and re-layouts, deliver(): by_kind[:, 1][:, flip_one]  28.9 us
    gather x2, local copies, waits for them, and re-layouts, per_device(): dpicked = candidates(out_cot, near_cot)[:, group_index, slot_kind]  26.1 us
    gather x2, local copies, waits for them, and re-layouts, per_device(): picked = candidates(tokens, near_tokens)[:, group_index, slot_kind]  25.7 us
    another operation x10, local copies, waits for them, and re-layouts, candidates(): return jnp.stack(stacked, axis=2)  25.1 us
  transfers between devices with their start and end apart: 12, of which 4 were waited for; matrix products, arithmetic and copies ran while one was open for 46% of the time, Pallas kernels for 0%

commit v1 on v0

v1 whole, which is shorter than its diff:
```python
import functools

import jax
import jax.numpy as jnp
from jax import lax
from jax.experimental import pallas as pl
from jax.experimental.pallas import tpu as pltpu
from jax.sharding import PartitionSpec as P

MESH = pl.DeviceIdType.MESH
F32, BF16 = jnp.float32, jnp.bfloat16
C = 4
J = 4
NB = 12
BLK = 256
TOK = 512
SIGNS = (1, -1)


def nn(a, b):
    return lax.dot_general(a, b, (((1,), (0,)), ((), ())), preferred_element_type=F32)


def nt(a, b):
    return lax.dot_general(a, b, (((1,), (1,)), ((), ())), preferred_element_type=F32)


def kernel(
    kept,
    tokens,
    out_cot,
    w_in,
    w_out,
    mixed,
    tokens_grad,
    w_in_grad,
    w_out_grad,
    g_in,
    g_out,
    t_in,
    t_out,
    r0,
    r1,
    r2,
    r3,
    zh_recv,
    z_send,
    z_recv,
    xs,
    cs,
    xt,
    acc_m,
    acc_n,
    far_send,
    far_recv,
    act_all,
    pg_all,
    ag_send_sem,
    ag_recv_sem,
    rs_send_sem,
    rs_recv_sem,
    zh_send_sem,
    zh_recv_sem,
    tok_send_sem,
    tok_recv_sem,
    far_send_sem,
    far_recv_sem,
    z_send_sem,
    z_recv_sem,
    local_sem,
):
    dp = lax.axis_index("dp")
    te = lax.axis_index("tensor")
    y, x, zh = dp // 8, (dp // 2) % 4, dp % 2
    scale = float(TOK * 32) ** -0.5

    def at(yy, xx, zz):
        return {"dp": (yy % 4) * 8 + (xx % 4) * 2 + zz}

    def beside(axis, d):
        return at(y, x + d + 4, zh) if axis == 0 else at(y + d + 4, x, zh)

    across = {"dp": dp + 1 - 2 * zh}
    core_peer = {"tensor": te + 1 - 2 * (te % 2)}
    z_peer = {"tensor": (te + 2) % 4}
    peers = (core_peer, z_peer)

    def remote(src, dst, send, recv, to):
        return pltpu.make_async_remote_copy(
            src_ref=src, dst_ref=dst, send_sem=send, recv_sem=recv, device_id=to, device_id_type=MESH
        )

    def load(kind, i):
        src, dst = ((tokens, xs), (out_cot, cs))[kind]
        return pltpu.make_async_copy(
            src.at[:, pl.ds(BLK * i, BLK)], dst.at[i], local_sem.at[kind, i]
        )

    for kind in range(2):
        for i in range(C):
            load(kind, i).start()

    barrier = pltpu.get_barrier_semaphore()
    everyone = [across, core_peer, z_peer] + [beside(a, d) for a in (0, 1) for d in SIGNS]
    for to in everyone:
        pl.semaphore_signal(barrier, inc=1, device_id=to, device_id_type=MESH)
    pl.semaphore_wait(barrier, len(everyone))

    def zh_copy(a):
        return remote(
            (w_in, w_out)[a], zh_recv.at[a], zh_send_sem.at[a], zh_recv_sem.at[a], across
        )

    for a in range(2):
        zh_copy(a).start()

    def tok_copy(kind, p, i):
        buf = (xs, cs)[kind]
        return remote(
            buf.at[i],
            buf.at[C * (p + 1) + i],
            tok_send_sem.at[kind, p, i],
            tok_recv_sem.at[kind, p, i],
            peers[p],
        )

    for kind in range(2):
        for i in range(C):
            load(kind, i).wait()

    for a in range(2):
        zh_copy(a).wait_recv()
        own = (w_in, w_out)[a][...].astype(F32).reshape(C, NB, 8, BLK)
        got = zh_recv[a].astype(F32).reshape(C, NB, 8, BLK)
        low = jnp.where(zh == 0, own, got)
        high = jnp.where(zh == 0, got, own)
        piece = jnp.concatenate([low, high], axis=2).astype(BF16)
        (g_in, g_out)[a][:, y, x] = piece

    def opposite(v, d):
        return (v - d + 4) % 4

    def half(d, n):
        return pl.ds(0, n // 2) if d == 1 else pl.ds(n // 2, n // 2)

    def ag_copy(a, c, stage, k):
        d = SIGNS[k]
        g = (g_in, g_out)[a].at[c]
        if stage == 0:
            ref, axis = g.at[y, x], a
        elif stage == 1:
            ref = (g.at[y, opposite(x, d)] if a == 0 else g.at[opposite(y, d), x]).at[half(d, NB)]
            axis = a
        elif stage == 2:
            ref, axis = (g.at[y] if a == 0 else g.at[:, x]), 1 - a
        else:
            ref = g.at[opposite(y, d), half(d, 4)] if a == 0 else g.at[half(d, 4), opposite(x, d)]
            axis = 1 - a
        return remote(
            ref, ref, ag_send_sem.at[a, c, stage, k], ag_recv_sem.at[a, c, stage, k], beside(axis, d)
        )

    def each(fn):
        for a in range(2):
            for k in range(2):
                fn(a, k)

    @pl.loop(0, C)
    def _(c):
        each(lambda a, k: ag_copy(a, c, 0, k).start())

    @pl.loop(0, C)
    def _(i):
        for kind in range(2):
            for p in range(2):
                tok_copy(kind, p, i).start()

    def transpose(i):
        xt[i] = xs[i].T

    @pl.loop(0, C)
    def _(i):
        transpose(i)

    @pl.loop(0, C)
    def _(c):
        def go(a, k):
            ag_copy(a, c, 0, k).wait_recv()
            ag_copy(a, c, 1, k).start()

        each(go)

    @pl.loop(0, C + 1)
    def _(c):
        @pl.when(c < C)
        def _():
            each(lambda a, k: ag_copy(a, c, 1, k).wait_recv())
            each(lambda a, k: ag_copy(a, c, 2, k).start())

        @pl.when(c >= 1)
        def _():
            def go(a, k):
                ag_copy(a, c - 1, 2, k).wait_recv()
                ag_copy(a, c - 1, 3, k).start()

            each(go)

    @pl.loop(0, C)
    def _(i):
        for kind in range(2):
            for p in range(2):
                tok_copy(kind, p, i).wait_recv()

    @pl.loop(C, 3 * C)
    def _(i):
        transpose(i)

    acc_m[...] = jnp.zeros_like(acc_m)
    acc_n[...] = jnp.zeros_like(acc_n)

    def rs_copy(a, c, stage, k):
        d = SIGNS[k]
        t = (t_in, t_out)[a].at[c]
        if stage == 0:
            src = t.at[(y + 2) % 4, half(d, 4)] if a == 0 else t.at[half(d, 4), (x + 2) % 4]
            dst, axis = r0, 1 - a
        elif stage == 1:
            src = t.at[(y + d + 4) % 4] if a == 0 else t.at[:, (x + d + 4) % 4]
            dst, axis = r1, 1 - a
        elif stage == 2:
            src = (t.at[y, (x + 2) % 4] if a == 0 else t.at[(y + 2) % 4, x]).at[half(d, NB)]
            dst, axis = r2, a
        else:
            src = t.at[y, (x + d + 4) % 4] if a == 0 else t.at[(y + d + 4) % 4, x]
            dst, axis = r3, a
        return remote(
            src,
            dst.at[a, c, k],
            rs_send_sem.at[a, c, stage, k],
            rs_recv_sem.at[a, c, stage, k],
            beside(axis, d),
        )

    def add(p, q):
        return p.astype(F32) + q.astype(F32)

    def rs_start(c):
        each(lambda a, k: rs_copy(a, c, 0, k).start())

    def rs_one(c):
        def go(a, k):
            d = SIGNS[k]
            rs_copy(a, c, 0, k).wait_recv()
            if a == 0:
                yy = (y + d + 4) % 4
                t_in[c, yy, half(d, 4)] = add(t_in[c, yy, half(d, 4)], r0[a, c, k]).astype(BF16)
            else:
                xx = (x + d + 4) % 4
                t_out[c, half(d, 4), xx] = add(t_out[c, half(d, 4), xx], r0[a, c, k]).astype(BF16)
            rs_copy(a, c, 1, k).start()

        each(go)

    def rs_two(c):
        for a in range(2):
            for k in range(2):
                rs_copy(a, c, 1, k).wait_recv()
            got = add(r1[a, c, 0], r1[a, c, 1])
            if a == 0:
                t_in[c, y] = (t_in[c, y].astype(F32) + got).astype(BF16)
            else:
                t_out[c, :, x] = (t_out[c, :, x].astype(F32) + got).astype(BF16)
            for k in range(2):
                rs_copy(a, c, 2, k).start()

    def rs_three(c):
        def go(a, k):
            d = SIGNS[k]
            rs_copy(a, c, 2, k).wait_recv()
            if a == 0:
                xx = (x + d + 4) % 4
                t_in[c, y, xx, half(d, NB)] = add(t_in[c, y, xx, half(d, NB)], r2[a, c, k]).astype(BF16)
            else:
                yy = (y + d + 4) % 4
                t_out[c, yy, x, half(d, NB)] = add(t_out[c, yy, x, half(d, NB)], r2[a, c, k]).astype(BF16)
            rs_copy(a, c, 3, k).start()

        each(go)

    def z_copy(a, c):
        return remote(
            z_send.at[a, c], z_recv.at[a, c], z_send_sem.at[a, c], z_recv_sem.at[a, c], across
        )

    def rs_four(c):
        for a in range(2):
            for k in range(2):
                rs_copy(a, c, 3, k).wait_recv()
            total = add(r3[a, c, 0], r3[a, c, 1]) + (t_in, t_out)[a][c, y, x].astype(F32)
            low, high = total[:, :8], total[:, 8:]
            mine = jnp.where(zh == 0, low, high)
            other = jnp.where(zh == 0, high, low)
            z_send[a, c] = other.reshape(NB * 8, BLK).astype(BF16)
            (w_in_grad, w_out_grad)[a][c] = mine
            z_copy(a, c).start()

    def rs_last(c):
        for a in range(2):
            z_copy(a, c).wait_recv()
            out = (w_in_grad, w_out_grad)[a]
            out[c] = out[c] + z_recv[a, c].astype(F32).reshape(NB, 8, BLK)

    def place(section, g):
        near = jnp.where(section == 0, g + 1 - 2 * (g % 2), (g + 2) % 4)
        far = jnp.where(section == 2, C + g, 2 * C + g)
        return jnp.where(section < 2, near, far)

    def block(ref, g, b):
        return ref[g, :, :, b].reshape(BLK, BLK)

    def part_one(g, j):
        h = J * g + j
        ids = [g, place(kept[h, 0], g), place(kept[h, 1], g)]
        ws = [block(g_in, g, 3 * j + s) for s in range(3)]
        pre = nn(xs[ids[0]], ws[0]) + nn(xs[ids[1]], ws[1]) + nn(xs[ids[2]], ws[2])
        cdf = 0.5 * (1.0 + lax.erf(pre * 0.7071067811865476))
        act = (pre * cdf).astype(BF16)
        slope = cdf + pre * jnp.exp(-0.5 * pre * pre) * 0.3989422804014327
        vs = [block(g_out, g, 3 * j + s) for s in range(3)]
        act_grad = nt(cs[ids[0]], vs[0]) + nt(cs[ids[1]], vs[1]) + nt(cs[ids[2]], vs[2])
        pg = (act_grad * slope).astype(BF16)
        act_all[j] = act
        pg_all[j] = pg
        act_t = act.T
        for s in range(3):
            out_term = (nn(act_t, cs[ids[s]]) * scale).astype(BF16)
            t_out[g, :, :, 3 * j + s] = out_term.reshape(4, 4, 16, BLK)
            in_term = (nn(xt[ids[s]], pg) * scale).astype(BF16)
            t_in[g, :, :, 3 * j + s] = in_term.reshape(4, 4, 16, BLK)

    def far_copy(kind, p, g):
        return remote(
            far_send.at[kind, p, g],
            far_recv.at[kind, p, g],
            far_send_sem.at[kind, p, g],
            far_recv_sem.at[kind, p, g],
            peers[p],
        )

    def part_two(g):
        def pick(ref, section):
            def one(j):
                h = J * g + j
                parts = []
                for s in range(2):
                    flag = jnp.where(kept[h, s] == section, 1.0, 0.0).astype(F32)
                    parts.append(block(ref, g, 3 * j + 1 + s).astype(F32) * flag)
                return (parts[0] + parts[1]).astype(BF16)

            return [one(j) for j in range(J)]

        def own(ref):
            return [block(ref, g, 3 * j) for j in range(J)]

        def total(kind, ws):
            if kind == 0:
                act = jnp.concatenate([act_all[j] for j in range(J)], axis=1)
                return nn(act, jnp.concatenate(ws, axis=0))
            pg = jnp.concatenate([pg_all[j] for j in range(J)], axis=1)
            return nt(pg, jnp.concatenate(ws, axis=1))

        for kind in range(2):
            ref = (g_out, g_in)[kind]
            acc = (acc_m, acc_n)[kind]
            for p in range(2):
                far_send[kind, p, g] = total(kind, pick(ref, 2 + p)).astype(BF16)
                far_copy(kind, p, g).start()
            acc[g] = acc[g] + total(kind, own(ref))
            near = (g + 1 - 2 * (g % 2), (g + 2) % 4)
            for p in range(2):
                acc[near[p]] = acc[near[p]] + total(kind, pick(ref, p))

    def wait_gather(c):
        each(lambda a, k: ag_copy(a, c, 3, k).wait_recv())

    @pl.loop(0, C + 3)
    def _(g):
        @pl.when(g < C)
        def _():
            wait_gather(g)

        def halfway(lo):
            @pl.when(g < C)
            def _():
                @pl.loop(lo, lo + 2)
                def _(j):
                    part_one(g, j)

        halfway(0)

        @pl.when((g >= 1) & (g < C + 1))
        def _():
            rs_one(g - 1)

        @pl.when((g >= 2) & (g < C + 2))
        def _():
            rs_three(g - 2)

        halfway(2)

        @pl.when(g < C)
        def _():
            part_two(g)

        @pl.when((g >= 1) & (g < C + 1))
        def _():
            rs_two(g - 1)

        @pl.when((g >= 2) & (g < C + 2))
        def _():
            rs_four(g - 2)

        @pl.when(g < C)
        def _():
            rs_start(g)

        @pl.when(g >= 3)
        def _():
            rs_last(g - 3)

    for kind in range(2):
        stage = (act_all, pg_all)[kind]
        out = (mixed, tokens_grad)[kind]
        for g in range(C):
            for p in range(2):
                far_copy(kind, p, g).wait_recv()
            value = (acc_m, acc_n)[kind][g] + add(far_recv[kind, 0, g], far_recv[kind, 1, g])
            stage[g] = value.astype(BF16)
            pltpu.make_async_copy(
                stage.at[g], out.at[:, pl.ds(BLK * g, BLK)], local_sem.at[kind, g]
            ).start()
    for kind in range(2):
        stage = (act_all, pg_all)[kind]
        out = (mixed, tokens_grad)[kind]
        for g in range(C):
            pltpu.make_async_copy(
                stage.at[g], out.at[:, pl.ds(BLK * g, BLK)], local_sem.at[kind, g]
            ).wait()

    for a in range(2):
        zh_copy(a).wait_send()

    @pl.loop(0, C)
    def _(c):
        for stage in range(4):
            each(lambda a, k: ag_copy(a, c, stage, k).wait_send())
            each(lambda a, k: rs_copy(a, c, stage, k).wait_send())
        for a in range(2):
            z_copy(a, c).wait_send()
            for p in range(2):
                tok_copy(a, p, c).wait_send()
                far_copy(a, p, c).wait_send()


def per_device(tokens, out_cot, kept, w_in, w_out):
    vmem = pl.BlockSpec(memory_space=pltpu.VMEM)
    hbm = pl.BlockSpec(memory_space=pl.ANY)
    dma = pltpu.SemaphoreType.DMA
    full = pltpu.VMEM((C, 4, 4, NB, 16, BLK), BF16)
    row = (TOK, BLK)
    mixed, tokens_grad, w_in_grad, w_out_grad = pl.pallas_call(
        kernel,
        out_shape=(
            jax.ShapeDtypeStruct(tokens.shape, BF16),
            jax.ShapeDtypeStruct(tokens.shape, BF16),
            jax.ShapeDtypeStruct((C, NB, 8, BLK), F32),
            jax.ShapeDtypeStruct((C, NB, 8, BLK), F32),
        ),
        in_specs=[pl.BlockSpec(memory_space=pltpu.SMEM), hbm, hbm, vmem, vmem],
        out_specs=(hbm, hbm, vmem, vmem),
        scratch_shapes=[
            full,
            full,
            full,
            full,
            pltpu.VMEM((2, C, 2, 2, NB, 16, BLK), BF16),
            pltpu.VMEM((2, C, 2, 4, NB, 16, BLK), BF16),
            pltpu.VMEM((2, C, 2, NB // 2, 16, BLK), BF16),
            pltpu.VMEM((2, C, 2, NB, 16, BLK), BF16),
            pltpu.VMEM((2, C * NB * 8, BLK), BF16),
            pltpu.VMEM((2, C, NB * 8, BLK), BF16),
            pltpu.VMEM((2, C, NB * 8, BLK), BF16),
            pltpu.VMEM((3 * C,) + row, BF16),
            pltpu.VMEM((3 * C,) + row, BF16),
            pltpu.VMEM((3 * C, BLK, TOK), BF16),
            pltpu.VMEM((C,) + row, F32),
            pltpu.VMEM((C,) + row, F32),
            pltpu.VMEM((2, 2, C) + row, BF16),
            pltpu.VMEM((2, 2, C) + row, BF16),
            pltpu.VMEM((J,) + row, BF16),
            pltpu.VMEM((J,) + row, BF16),
            dma((2, C, 4, 2)),
            dma((2, C, 4, 2)),
            dma((2, C, 4, 2)),
            dma((2, C, 4, 2)),
            dma((2,)),
            dma((2,)),
            dma((2, 2, C)),
            dma((2, 2, C)),
            dma((2, 2, C)),
            dma((2, 2, C)),
            dma((2, C)),
            dma((2, C)),
            dma((2, C)),
        ],
        compiler_params=pltpu.CompilerParams(
            collective_id=0, has_side_effects=True, vmem_limit_bytes=64 * 2**20
        ),
        cost_estimate=pl.CostEstimate(
            flops=24 * 10**9, bytes_accessed=8 * 2**20, transcendentals=4 * 2**20
        ),
    )(kept, tokens, out_cot, w_in.reshape(C * NB * 8, BLK), w_out.reshape(C * NB * 8, BLK))
    shape = w_in.shape
    return mixed, tokens_grad, w_in_grad.reshape(shape), w_out_grad.reshape(shape)


def solution(mesh):
    wide, blocks = P("dp", "tensor"), P("tensor", None, "dp", None)
    return jax.shard_map(
        per_device,
        mesh=mesh,
        in_specs=(wide, wide, P("tensor", None), blocks, blocks),
        out_specs=(wide, wide, blocks, blocks),
        check_vma=False,
    )
```

time: 782 us -> 183 us (0.23); the launches traced: 771 us -> 183 us
  waiting for transfers between devices: 347 us -> 0 us
  local copies, waits for them, and re-layouts: 207 us -> 6.82 us
  matrix products: 188 us -> 0 us
  Pallas kernels: 0 us -> 175 us
  between operations: 14.5 us -> 0.66 us
  other arithmetic: 8.67 us -> 0 us
    reduce_scatter x1 -> x0, waiting for transfers between devices: 226 us -> none  [per_device(): lax.psum_scatter(out_term.astype(jnp.bfloat16), 'dp', scatter_dimension=2...]
    dot_general x8 -> x0, matrix products: 188 us -> none  [the longest x2 101 us: deliver(): jnp.einsum('tgjso,gjsk->tkgo', grouped, kind_mask, precision=lax.Precisio...]
    pallas_call x0 -> x1, Pallas kernels: none -> 175 us  [per_device(): pl.pallas_call(kernel, out_shape=(jax.ShapeDtypeStruct(tokens.shape, BF16...]
    all_gather x2 -> x0, waiting for transfers between devices: 96.9 us -> none  [the longest x1 88.7 us: per_device(): lax.all_gather(w_out, 'dp', axis=2, tiled=True)]
    gather x12 -> x0, local copies, waits for them, and re-layouts: 65.7 us -> none  [the longest x2 26.1 us: per_device(): dpicked = candidates(out_cot, near_cot)[:, group_index, slot_kind]]
    unnamed x50 -> x13, local copies, waits for them, and re-layouts: 60.5 us -> 6.82 us
    slice x4 -> x0, local copies, waits for them, and re-layouts: 42.7 us -> none  [the longest x2 28.9 us: deliver(): by_kind[:, 1][:, flip_one]]
    another operation x10 -> x0, local copies, waits for them, and re-layouts: 25.1 us -> none  [candidates(): return jnp.stack(stacked, axis=2)]
  transfers between devices with their start and end apart: 12 -> 0, of which waited for: 4 -> 0; matrix products, arithmetic and copies ran while one was open for 46% -> 0% of each run, Pallas kernels for 0% -> 0%
where the time goes in v1:
time: 183 us
  Pallas kernels  175 us (96%)
  local copies, waits for them, and re-layouts  6.82 us (4%)
    pallas_call x1, Pallas kernels, per_device(): pl.pallas_call(kernel, out_shape=(jax.ShapeDtypeStruct(tokens.shape, BF16...  175 us
    unnamed x13, local copies, waits for them, and re-layouts  6.82 us

profile of v1, /device:TPU:0, one launch (start us, length us, event | category | flops | bytes accessed | tf_op | source)
XLA Modules:
  0.0 182.9 jit_solution(8742924082375253574)
XLA Ops:
  0.6 0.0 copy-start.3
  0.6 0.7 copy-done.3
  1.3 0.7 copy.9.kept
  2.0 175.4 %shard_map.84 = (bf16[512,1024]{1,0:T(8,128)(2,1)}, bf16[512,1024]{1,0:T(8,128)(2,1)}, f32[4,12,8,256]{3,2,1,0:T(8,128)}, f32[4,12,8,256]{3,2,1,0:T(8,128)}) custom-call(s32[16,2]{1,0:T(8,128)} %copy.9.kept, bf16[512,1024]{1,0:T(8,128)(2,1)} %tokens.1, bf16[512,1024]{1,0:T(8,128)(2,1)} %out_cot.1, bf16[384,256]{1,0:T(8,128)(2,1)} %bitcast.6, ...), custom_call_target="tpu_custom_call" | custom-call | flops 24000000000 | bytes 8388608 | tf_op jit(solution)/shard_map/pallas_call | solution.py:471
  177.4 0.0 copy-start
  177.5 2.4 %copy.14 = bf16[512,1024]{1,0:T(8,128)(2,1)} copy(bf16[512,1024]{1,0:T(8,128)(2,1)} %get-tuple-element.16) | data formatting | bytes 2097152
  179.8 0.0 copy-done
  179.8 0.0 copy-start.2
  179.8 1.0 copy.15
  180.8 0.3 copy-done.2
  181.0 0.0 copy-start.1
  181.0 0.7 copy.16
  181.8 0.4 copy-done.1
  182.2 0.7 copy.17
Async XLA Ops:
  0.6 0.7 copy-start.3
  177.4 2.4 %copy-start = (bf16[512,1024]{1,0:T(8,128)(2,1)S(1)}, bf16[512,1024]{1,0:T(8,128)(2,1)}, u32[]{:S(2)}) copy-start(bf16[512,1024]{1,0:T(8,128)(2,1)} %get-tuple-element.17) | copy-start | bytes 3145732
  179.8 1.2 copy-start.2
  181.0 1.1 copy-start.1

commit v2 on v1

--- a/solution.py
+++ b/solution.py
@@ -106,13 +106,19 @@
         pl.semaphore_signal(barrier, inc=1, device_id=to, device_id_type=MESH)
     pl.semaphore_wait(barrier, len(everyone))
 
-    def zh_copy(a):
+    def zh_copy(a, c):
+        rows = pl.ds(c * NB * 8, NB * 8)
         return remote(
-            (w_in, w_out)[a], zh_recv.at[a], zh_send_sem.at[a], zh_recv_sem.at[a], across
-        )
-
-    for a in range(2):
-        zh_copy(a).start()
+            (w_in, w_out)[a].at[rows],
+            zh_recv.at[a, rows],
+            zh_send_sem.at[a, c],
+            zh_recv_sem.at[a, c],
+            across,
+        )
+
+    for c in range(C):
+        for a in range(2):
+            zh_copy(a, c).start()
 
     def tok_copy(kind, p, i):
         buf = (xs, cs)[kind]
@@ -128,14 +134,14 @@
         for i in range(C):
             load(kind, i).wait()
 
-    for a in range(2):
-        zh_copy(a).wait_recv()
-        own = (w_in, w_out)[a][...].astype(F32).reshape(C, NB, 8, BLK)
-        got = zh_recv[a].astype(F32).reshape(C, NB, 8, BLK)
+    def join(a, c):
+        rows = pl.ds(c * NB * 8, NB * 8)
+        zh_copy(a, c).wait_recv()
+        own = (w_in, w_out)[a][rows].astype(F32).reshape(NB, 8, BLK)
+        got = zh_recv[a, rows].astype(F32).reshape(NB, 8, BLK)
         low = jnp.where(zh == 0, own, got)
         high = jnp.where(zh == 0, got, own)
-        piece = jnp.concatenate([low, high], axis=2).astype(BF16)
-        (g_in, g_out)[a][:, y, x] = piece
+        (g_in, g_out)[a][c, y, x] = jnp.concatenate([low, high], axis=1).astype(BF16)
 
     def opposite(v, d):
         return (v - d + 4) % 4
@@ -167,13 +173,13 @@
 
     @pl.loop(0, C)
     def _(c):
-        each(lambda a, k: ag_copy(a, c, 0, k).start())
-
-    @pl.loop(0, C)
-    def _(i):
+        for a in range(2):
+            join(a, c)
+            for k in range(2):
+                ag_copy(a, c, 0, k).start()
         for kind in range(2):
             for p in range(2):
-                tok_copy(kind, p, i).start()
+                tok_copy(kind, p, c).start()
 
     def transpose(i):
         xt[i] = xs[i].T
@@ -190,20 +196,21 @@
 
         each(go)
 
-    @pl.loop(0, C + 1)
+    def ag_three(c):
+        def go(a, k):
+            ag_copy(a, c, 2, k).wait_recv()
+            ag_copy(a, c, 3, k).start()
+
+        each(go)
+
+    @pl.loop(0, C)
     def _(c):
-        @pl.when(c < C)
-        def _():
-            each(lambda a, k: ag_copy(a, c, 1, k).wait_recv())
-            each(lambda a, k: ag_copy(a, c, 2, k).start())
+        each(lambda a, k: ag_copy(a, c, 1, k).wait_recv())
+        each(lambda a, k: ag_copy(a, c, 2, k).start())
 
         @pl.when(c >= 1)
         def _():
-            def go(a, k):
-                ag_copy(a, c - 1, 2, k).wait_recv()
-                ag_copy(a, c - 1, 3, k).start()
-
-            each(go)
+            ag_three(c - 1)
 
     @pl.loop(0, C)
     def _(i):
@@ -383,72 +390,58 @@
     def wait_gather(c):
         each(lambda a, k: ag_copy(a, c, 3, k).wait_recv())
 
-    @pl.loop(0, C + 3)
+    def finish():
+        def out_copy(kind, g):
+            stage = (act_all, pg_all)[kind]
+            out = (mixed, tokens_grad)[kind]
+            return pltpu.make_async_copy(
+                stage.at[g], out.at[:, pl.ds(BLK * g, BLK)], local_sem.at[kind, g]
+            )
+
+        for kind in range(2):
+            for g in range(C):
+                for p in range(2):
+                    far_copy(kind, p, g).wait_recv()
+                value = (acc_m, acc_n)[kind][g] + add(far_recv[kind, 0, g], far_recv[kind, 1, g])
+                (act_all, pg_all)[kind][g] = value.astype(BF16)
+                out_copy(kind, g).start()
+        for kind in range(2):
+            for g in range(C):
+                out_copy(kind, g).wait()
+
+    def event(g, behind, fn):
+        @pl.when((g >= behind) & (g < C + behind))
+        def _():
+            fn(g - behind)
+
+    def compute(g):
+        wait_gather(g)
+
+        @pl.loop(0, J)
+        def _(j):
+            part_one(g, j)
+
+        part_two(g)
+
+    @pl.loop(0, C + 5)
     def _(g):
-        @pl.when(g < C)
+        event(g, 0, compute)
+
+        @pl.when(g == 0)
         def _():
-            wait_gather(g)
-
-        def halfway(lo):
-            @pl.when(g < C)
-            def _():
-                @pl.loop(lo, lo + 2)
-                def _(j):
-                    part_one(g, j)
-
-        halfway(0)
-
-        @pl.when((g >= 1) & (g < C + 1))
+            ag_three(C - 1)
+
+        event(g, 0, rs_start)
+        event(g, 1, rs_one)
+        event(g, 3, rs_three)
+        event(g, 4, rs_four)
+
+        @pl.when(g == C + 1)
         def _():
-            rs_one(g - 1)
-
-        @pl.when((g >= 2) & (g < C + 2))
-        def _():
-            rs_three(g - 2)
-
-        halfway(2)
-
-        @pl.when(g < C)
-        def _():
-            part_two(g)
-
-        @pl.when((g >= 1) & (g < C + 1))
-        def _():
-            rs_two(g - 1)
-
-        @pl.when((g >= 2) & (g < C + 2))
-        def _():
-            rs_four(g - 2)
-
-        @pl.when(g < C)
-        def _():
-            rs_start(g)
-
-        @pl.when(g >= 3)
-        def _():
-            rs_last(g - 3)
-
-    for kind in range(2):
-        stage = (act_all, pg_all)[kind]
-        out = (mixed, tokens_grad)[kind]
-        for g in range(C):
-            for p in range(2):
-                far_copy(kind, p, g).wait_recv()
-            value = (acc_m, acc_n)[kind][g] + add(far_recv[kind, 0, g], far_recv[kind, 1, g])
-            stage[g] = value.astype(BF16)
-            pltpu.make_async_copy(
-                stage.at[g], out.at[:, pl.ds(BLK * g, BLK)], local_sem.at[kind, g]
-            ).start()
-    for kind in range(2):
-        stage = (act_all, pg_all)[kind]
-        out = (mixed, tokens_grad)[kind]
-        for g in range(C):
-            pltpu.make_async_copy(
-                stage.at[g], out.at[:, pl.ds(BLK * g, BLK)], local_sem.at[kind, g]
-            ).wait()
-
-    for a in range(2):
-        zh_copy(a).wait_send()
+            finish()
+
+        event(g, 2, rs_two)
+        event(g, 5, rs_last)
 
     @pl.loop(0, C)
     def _(c):
@@ -456,10 +449,35 @@
             each(lambda a, k: ag_copy(a, c, stage, k).wait_send())
             each(lambda a, k: rs_copy(a, c, stage, k).wait_send())
         for a in range(2):
+            zh_copy(a, c).wait_send()
             z_copy(a, c).wait_send()
             for p in range(2):
                 tok_copy(a, p, c).wait_send()
                 far_copy(a, p, c).wait_send()
+
+
+def hand_over(*refs):
+    n = 4
+    ins, outs, bufs, (sem_in, sem_out) = refs[:n], refs[n : 2 * n], refs[2 * n : 3 * n], refs[3 * n :]
+    copies = []
+    for i in range(n):
+        parts = 4 if i < 2 else 1
+        rows = ins[i].shape[0] // parts
+        for k in range(parts):
+            at = pl.ds(k * rows, rows)
+            copies.append(
+                (
+                    pltpu.make_async_copy(ins[i].at[at], bufs[i].at[at], sem_in.at[i, k]),
+                    pltpu.make_async_copy(bufs[i].at[at], outs[i].at[at], sem_out.at[i, k]),
+                )
+            )
+    for first, _ in copies:
+        first.start()
+    for first, second in copies:
+        first.wait()
+        second.start()
+    for _, second in copies:
+        second.wait()
 
 
 def per_device(tokens, out_cot, kept, w_in, w_out):
@@ -468,7 +486,7 @@
     dma = pltpu.SemaphoreType.DMA
     full = pltpu.VMEM((C, 4, 4, NB, 16, BLK), BF16)
     row = (TOK, BLK)
-    mixed, tokens_grad, w_in_grad, w_out_grad = pl.pallas_call(
+    results = pl.pallas_call(
         kernel,
         out_shape=(
             jax.ShapeDtypeStruct(tokens.shape, BF16),
@@ -503,8 +521,8 @@
             dma((2, C, 4, 2)),
             dma((2, C, 4, 2)),
             dma((2, C, 4, 2)),
-            dma((2,)),
-            dma((2,)),
+            dma((2, C)),
+            dma((2, C)),
             dma((2, 2, C)),
             dma((2, 2, C)),
             dma((2, 2, C)),
@@ -520,6 +538,13 @@
             flops=24 * 10**9, bytes_accessed=8 * 2**20, transcendentals=4 * 2**20
         ),
     )(kept, tokens, out_cot, w_in.reshape(C * NB * 8, BLK), w_out.reshape(C * NB * 8, BLK))
+    mixed, tokens_grad, w_in_grad, w_out_grad = pl.pallas_call(
+        hand_over,
+        out_shape=tuple(jax.ShapeDtypeStruct(r.shape, r.dtype) for r in results),
+        in_specs=[hbm] * 4,
+        out_specs=(hbm,) * 4,
+        scratch_shapes=[pltpu.VMEM(r.shape, r.dtype) for r in results] + [dma((4, 4)), dma((4, 4))],
+    )(*results)
     shape = w_in.shape
     return mixed, tokens_grad, w_in_grad.reshape(shape), w_out_grad.reshape(shape)
 

time: 183 us -> 162 us (0.89)
  Pallas kernels: 175 us -> 160 us
  local copies, waits for them, and re-layouts: 6.82 us -> 1.35 us
    pallas_call x1, Pallas kernels: 175 us -> 157 us  [per_device(): pl.pallas_call(kernel, out_shape=(jax.ShapeDtypeStruct(tokens.shape, BF16...]
    unnamed x13 -> x3, local copies, waits for them, and re-layouts: 6.82 us -> 1.35 us
    pallas_call x0 -> x1, Pallas kernels: none -> 2.8 us  [per_device(): pl.pallas_call(hand_over, out_shape=tuple((jax.ShapeDtypeStruct(r.shape,...]
where the time goes in v2:
time: 162 us
  Pallas kernels  160 us (99%)
    pallas_call x1, Pallas kernels, per_device(): pl.pallas_call(kernel, out_shape=(jax.ShapeDtypeStruct(tokens.shape, BF16...  157 us

profile of v2, /device:TPU:0, one launch (start us, length us, event | category | flops | bytes accessed | tf_op | source)
XLA Modules:
  0.0 161.8 jit_solution(8835581752479907481)
XLA Ops:
  0.6 0.0 copy-start
  0.6 0.7 copy-done
  1.3 0.7 copy.9.kept
  2.0 157.0 %shard_map.84 = (bf16[512,1024]{1,0:T(8,128)(2,1)}, bf16[512,1024]{1,0:T(8,128)(2,1)}, f32[4,12,8,256]{3,2,1,0:T(8,128)}, f32[4,12,8,256]{3,2,1,0:T(8,128)}) custom-call(s32[16,2]{1,0:T(8,128)} %copy.9.kept, bf16[512,1024]{1,0:T(8,128)(2,1)} %tokens.1, bf16[512,1024]{1,0:T(8,128)(2,1)} %out_cot.1, bf16[384,256]{1,0:T(8,128)(2,1)} %bitcast.6, ...), custom_call_target="tpu_custom_call" | custom-call | flops 24000000000 | bytes 8388608 | tf_op jit(solution)/shard_map/pallas_call | solution.py:489
  159.0 2.8 %shard_map.85 = (bf16[512,1024]{1,0:T(8,128)(2,1)}, bf16[512,1024]{1,0:T(8,128)(2,1)}, f32[4,12,8,256]{3,2,1,0:T(8,128)}, f32[4,12,8,256]{3,2,1,0:T(8,128)}) custom-call(bf16[512,1024]{1,0:T(8,128)(2,1)} %get-tuple-element.12.refs_0_, bf16[512,1024]{1,0:T(8,128)(2,1)} %get-tuple-element.13.refs_1_, f32[4,12,8,256]{3,2,1,0:T(8,128)} %get-tuple-element.14.refs_2_, ...), custom_call_target="tpu_custom_call" | custom-call | tf_op jit(solution)/shard_map/pallas_call | solution.py:541
Async XLA Ops:
  0.6 0.7 copy-start

commit v3 on v2

--- a/solution.py
+++ b/solution.py
@@ -12,6 +12,9 @@
 C = 4
 J = 4
 NB = 12
+R = 2 * C
+RB = NB // 2
+EARLY = 3
 BLK = 256
 TOK = 512
 SIGNS = (1, -1)
@@ -49,6 +52,9 @@
     xs,
     cs,
     xt,
+    xs_far,
+    cs_far,
+    xt_far,
     acc_m,
     acc_n,
     far_send,
@@ -121,10 +127,9 @@
             zh_copy(a, c).start()
 
     def tok_copy(kind, p, i):
-        buf = (xs, cs)[kind]
         return remote(
-            buf.at[i],
-            buf.at[C * (p + 1) + i],
+            (xs, cs)[kind].at[i],
+            (xs_far, cs_far)[kind].at[p, i],
             tok_send_sem.at[kind, p, i],
             tok_recv_sem.at[kind, p, i],
             peers[p],
@@ -136,7 +141,6 @@
 
     def join(a, c):
         rows = pl.ds(c * NB * 8, NB * 8)
-        zh_copy(a, c).wait_recv()
         own = (w_in, w_out)[a][rows].astype(F32).reshape(NB, 8, BLK)
         got = zh_recv[a, rows].astype(F32).reshape(NB, 8, BLK)
         low = jnp.where(zh == 0, own, got)
@@ -171,9 +175,12 @@
             for k in range(2):
                 fn(a, k)
 
-    @pl.loop(0, C)
-    def _(c):
-        for a in range(2):
+    def transpose(i):
+        xt[i] = xs[i].T
+
+    def ag_zero(c):
+        for a in range(2):
+            zh_copy(a, c).wait_recv()
             join(a, c)
             for k in range(2):
                 ag_copy(a, c, 0, k).start()
@@ -181,46 +188,31 @@
             for p in range(2):
                 tok_copy(kind, p, c).start()
 
-    def transpose(i):
-        xt[i] = xs[i].T
-
-    @pl.loop(0, C)
-    def _(i):
-        transpose(i)
-
-    @pl.loop(0, C)
-    def _(c):
-        def go(a, k):
-            ag_copy(a, c, 0, k).wait_recv()
-            ag_copy(a, c, 1, k).start()
-
-        each(go)
-
-    def ag_three(c):
-        def go(a, k):
-            ag_copy(a, c, 2, k).wait_recv()
-            ag_copy(a, c, 3, k).start()
-
-        each(go)
-
-    @pl.loop(0, C)
-    def _(c):
-        each(lambda a, k: ag_copy(a, c, 1, k).wait_recv())
-        each(lambda a, k: ag_copy(a, c, 2, k).start())
-
-        @pl.when(c >= 1)
+    def ag_next(stage):
+        def go(c):
+            for a in range(2):
+                for k in range(2):
+                    ag_copy(a, c, stage - 1, k).wait_recv()
+                    if stage != 2:
+                        ag_copy(a, c, stage, k).start()
+                if stage == 2:
+                    for k in range(2):
+                        ag_copy(a, c, stage, k).start()
+
+        return go
+
+    def event(t, behind, fn, count=C):
+        @pl.when((t >= behind) & (t < count + behind))
         def _():
-            ag_three(c - 1)
-
-    @pl.loop(0, C)
-    def _(i):
-        for kind in range(2):
-            for p in range(2):
-                tok_copy(kind, p, i).wait_recv()
-
-    @pl.loop(C, 3 * C)
-    def _(i):
-        transpose(i)
+            fn(t - behind)
+
+    @pl.loop(0, C + 2)
+    def _(t):
+        event(t, 0, ag_zero)
+        event(t, 1, ag_next(1))
+        event(t, 2, ag_next(2))
+        event(t, 3, ag_next(3), EARLY)
+        event(t, 0, transpose)
 
     acc_m[...] = jnp.zeros_like(acc_m)
     acc_n[...] = jnp.zeros_like(acc_n)
@@ -235,7 +227,7 @@
             src = t.at[(y + d + 4) % 4] if a == 0 else t.at[:, (x + d + 4) % 4]
             dst, axis = r1, 1 - a
         elif stage == 2:
-            src = (t.at[y, (x + 2) % 4] if a == 0 else t.at[(y + 2) % 4, x]).at[half(d, NB)]
+            src = (t.at[y, (x + 2) % 4] if a == 0 else t.at[(y + 2) % 4, x]).at[half(d, RB)]
             dst, axis = r2, a
         else:
             src = t.at[y, (x + d + 4) % 4] if a == 0 else t.at[(y + d + 4) % 4, x]
@@ -286,10 +278,10 @@
             rs_copy(a, c, 2, k).wait_recv()
             if a == 0:
                 xx = (x + d + 4) % 4
-                t_in[c, y, xx, half(d, NB)] = add(t_in[c, y, xx, half(d, NB)], r2[a, c, k]).astype(BF16)
+                t_in[c, y, xx, half(d, RB)] = add(t_in[c, y, xx, half(d, RB)], r2[a, c, k]).astype(BF16)
             else:
                 yy = (y + d + 4) % 4
-                t_out[c, yy, x, half(d, NB)] = add(t_out[c, yy, x, half(d, NB)], r2[a, c, k]).astype(BF16)
+                t_out[c, yy, x, half(d, RB)] = add(t_out[c, yy, x, half(d, RB)], r2[a, c, k]).astype(BF16)
             rs_copy(a, c, 3, k).start()
 
         each(go)
@@ -307,7 +299,7 @@
             low, high = total[:, :8], total[:, 8:]
             mine = jnp.where(zh == 0, low, high)
             other = jnp.where(zh == 0, high, low)
-            z_send[a, c] = other.reshape(NB * 8, BLK).astype(BF16)
+            z_send[a, c] = other.reshape(RB * 8, BLK).astype(BF16)
             (w_in_grad, w_out_grad)[a][c] = mine
             z_copy(a, c).start()
 
@@ -315,35 +307,39 @@
         for a in range(2):
             z_copy(a, c).wait_recv()
             out = (w_in_grad, w_out_grad)[a]
-            out[c] = out[c] + z_recv[a, c].astype(F32).reshape(NB, 8, BLK)
-
-    def place(section, g):
-        near = jnp.where(section == 0, g + 1 - 2 * (g % 2), (g + 2) % 4)
-        far = jnp.where(section == 2, C + g, 2 * C + g)
-        return jnp.where(section < 2, near, far)
+            out[c] = out[c] + z_recv[a, c].astype(F32).reshape(RB, 8, BLK)
+
+    def choose(near, far, section, g):
+        other = jnp.where(section == 0, g + 1 - 2 * (g % 2), (g + 2) % 4)
+        return jnp.where(
+            section < 2, near[other], jnp.where(section == 2, far[0, g], far[1, g])
+        )
 
     def block(ref, g, b):
         return ref[g, :, :, b].reshape(BLK, BLK)
 
     def part_one(g, j):
         h = J * g + j
-        ids = [g, place(kept[h, 0], g), place(kept[h, 1], g)]
+        x_s, c_s, t_s = [
+            [near[g]] + [choose(near, far, kept[s, h], g) for s in range(2)]
+            for near, far in ((xs, xs_far), (cs, cs_far), (xt, xt_far))
+        ]
         ws = [block(g_in, g, 3 * j + s) for s in range(3)]
-        pre = nn(xs[ids[0]], ws[0]) + nn(xs[ids[1]], ws[1]) + nn(xs[ids[2]], ws[2])
+        pre = nn(x_s[0], ws[0]) + nn(x_s[1], ws[1]) + nn(x_s[2], ws[2])
         cdf = 0.5 * (1.0 + lax.erf(pre * 0.7071067811865476))
         act = (pre * cdf).astype(BF16)
         slope = cdf + pre * jnp.exp(-0.5 * pre * pre) * 0.3989422804014327
         vs = [block(g_out, g, 3 * j + s) for s in range(3)]
-        act_grad = nt(cs[ids[0]], vs[0]) + nt(cs[ids[1]], vs[1]) + nt(cs[ids[2]], vs[2])
+        act_grad = nt(c_s[0], vs[0]) + nt(c_s[1], vs[1]) + nt(c_s[2], vs[2])
         pg = (act_grad * slope).astype(BF16)
         act_all[j] = act
         pg_all[j] = pg
         act_t = act.T
         for s in range(3):
-            out_term = (nn(act_t, cs[ids[s]]) * scale).astype(BF16)
-            t_out[g, :, :, 3 * j + s] = out_term.reshape(4, 4, 16, BLK)
-            in_term = (nn(xt[ids[s]], pg) * scale).astype(BF16)
-            t_in[g, :, :, 3 * j + s] = in_term.reshape(4, 4, 16, BLK)
+            out_term = (nn(act_t, c_s[s]) * scale).astype(BF16)
+            t_out[2 * g + j // 2, :, :, 3 * (j % 2) + s] = out_term.reshape(4, 4, 16, BLK)
+            in_term = (nn(t_s[s], pg) * scale).astype(BF16)
+            t_in[2 * g + j // 2, :, :, 3 * (j % 2) + s] = in_term.reshape(4, 4, 16, BLK)
 
     def far_copy(kind, p, g):
         return remote(
@@ -360,7 +356,7 @@
                 h = J * g + j
                 parts = []
                 for s in range(2):
-                    flag = jnp.where(kept[h, s] == section, 1.0, 0.0).astype(F32)
+                    flag = jnp.where(kept[s, h] == section, 1.0, 0.0).astype(F32)
                     parts.append(block(ref, g, 3 * j + 1 + s).astype(F32) * flag)
                 return (parts[0] + parts[1]).astype(BF16)
 
@@ -402,6 +398,7 @@
             for g in range(C):
                 for p in range(2):
                     far_copy(kind, p, g).wait_recv()
+                    far_copy(kind, p, g).wait_send()
                 value = (acc_m, acc_n)[kind][g] + add(far_recv[kind, 0, g], far_recv[kind, 1, g])
                 (act_all, pg_all)[kind][g] = value.astype(BF16)
                 out_copy(kind, g).start()
@@ -409,51 +406,63 @@
             for g in range(C):
                 out_copy(kind, g).wait()
 
-    def event(g, behind, fn):
-        @pl.when((g >= behind) & (g < C + behind))
+    def compute(u):
+        g = u // 2
+
+        @pl.when(u % 2 == 0)
         def _():
-            fn(g - behind)
-
-    def compute(g):
-        wait_gather(g)
-
-        @pl.loop(0, J)
+            for kind in range(2):
+                for p in range(2):
+                    tok_copy(kind, p, g).wait_recv()
+            for p in range(2):
+                xt_far[p, g] = xs_far[p, g].T
+            wait_gather(g)
+
+        @pl.loop(2 * (u % 2), 2 * (u % 2) + 2)
         def _(j):
             part_one(g, j)
 
-        part_two(g)
-
-    @pl.loop(0, C + 5)
-    def _(g):
-        event(g, 0, compute)
-
-        @pl.when(g == 0)
+    def compute_two(u):
+        @pl.when(u % 2 == 1)
         def _():
-            ag_three(C - 1)
-
-        event(g, 0, rs_start)
-        event(g, 1, rs_one)
-        event(g, 3, rs_three)
-        event(g, 4, rs_four)
-
-        @pl.when(g == C + 1)
+            part_two(u // 2)
+
+    def gather_sent(c):
+        for stage in range(4):
+            each(lambda a, k: ag_copy(a, c, stage, k).wait_send())
+        for a in range(2):
+            zh_copy(a, c).wait_send()
+            for p in range(2):
+                tok_copy(a, p, c).wait_send()
+
+    def scatter_sent(c):
+        for stage in range(4):
+            each(lambda a, k: rs_copy(a, c, stage, k).wait_send())
+        for a in range(2):
+            z_copy(a, c).wait_send()
+
+    @pl.loop(0, R + 6)
+    def _(u):
+        event(u, 0, compute, R)
+
+        @pl.when((u % 2 == 1) & (u < 2 * (C - EARLY)))
+        def _():
+            ag_next(3)(EARLY + u // 2)
+
+        event(u, 0, rs_start, R)
+        event(u, 2, rs_one, R)
+        event(u, 0, compute_two, R)
+        event(u, 4, rs_three, R)
+        event(u, 5, rs_four, R)
+
+        @pl.when(u == R + 2)
         def _():
             finish()
 
-        event(g, 2, rs_two)
-        event(g, 5, rs_last)
-
-    @pl.loop(0, C)
-    def _(c):
-        for stage in range(4):
-            each(lambda a, k: ag_copy(a, c, stage, k).wait_send())
-            each(lambda a, k: rs_copy(a, c, stage, k).wait_send())
-        for a in range(2):
-            zh_copy(a, c).wait_send()
-            z_copy(a, c).wait_send()
-            for p in range(2):
-                tok_copy(a, p, c).wait_send()
-                far_copy(a, p, c).wait_send()
+        event(u, 3, rs_two, R)
+        event(u, 6, rs_last, R)
+        event(u, 6, scatter_sent, R)
+        event(u, 4, gather_sent)
 
 
 def hand_over(*refs):
@@ -485,32 +494,36 @@
     hbm = pl.BlockSpec(memory_space=pl.ANY)
     dma = pltpu.SemaphoreType.DMA
     full = pltpu.VMEM((C, 4, 4, NB, 16, BLK), BF16)
+    term = pltpu.VMEM((R, 4, 4, RB, 16, BLK), BF16)
     row = (TOK, BLK)
     results = pl.pallas_call(
         kernel,
         out_shape=(
             jax.ShapeDtypeStruct(tokens.shape, BF16),
             jax.ShapeDtypeStruct(tokens.shape, BF16),
-            jax.ShapeDtypeStruct((C, NB, 8, BLK), F32),
-            jax.ShapeDtypeStruct((C, NB, 8, BLK), F32),
+            jax.ShapeDtypeStruct((R, RB, 8, BLK), F32),
+            jax.ShapeDtypeStruct((R, RB, 8, BLK), F32),
         ),
         in_specs=[pl.BlockSpec(memory_space=pltpu.SMEM), hbm, hbm, vmem, vmem],
         out_specs=(hbm, hbm, vmem, vmem),
         scratch_shapes=[
             full,
             full,
-            full,
-            full,
-            pltpu.VMEM((2, C, 2, 2, NB, 16, BLK), BF16),
-            pltpu.VMEM((2, C, 2, 4, NB, 16, BLK), BF16),
-            pltpu.VMEM((2, C, 2, NB // 2, 16, BLK), BF16),
-            pltpu.VMEM((2, C, 2, NB, 16, BLK), BF16),
+            term,
+            term,
+            pltpu.VMEM((2, R, 2, 2, RB, 16, BLK), BF16),
+            pltpu.VMEM((2, R, 2, 4, RB, 16, BLK), BF16),
+            pltpu.VMEM((2, R, 2, RB // 2, 16, BLK), BF16),
+            pltpu.VMEM((2, R, 2, RB, 16, BLK), BF16),
             pltpu.VMEM((2, C * NB * 8, BLK), BF16),
-            pltpu.VMEM((2, C, NB * 8, BLK), BF16),
-            pltpu.VMEM((2, C, NB * 8, BLK), BF16),
-            pltpu.VMEM((3 * C,) + row, BF16),
-            pltpu.VMEM((3 * C,) + row, BF16),
-            pltpu.VMEM((3 * C, BLK, TOK), BF16),
+            pltpu.VMEM((2, R, RB * 8, BLK), BF16),
+            pltpu.VMEM((2, R, RB * 8, BLK), BF16),
+            pltpu.VMEM((C,) + row, BF16),
+            pltpu.VMEM((C,) + row, BF16),
+            pltpu.VMEM((C, BLK, TOK), BF16),
+            pltpu.VMEM((2, C) + row, BF16),
+            pltpu.VMEM((2, C) + row, BF16),
+            pltpu.VMEM((2, C, BLK, TOK), BF16),
             pltpu.VMEM((C,) + row, F32),
             pltpu.VMEM((C,) + row, F32),
             pltpu.VMEM((2, 2, C) + row, BF16),
@@ -519,16 +532,16 @@
             pltpu.VMEM((J,) + row, BF16),
             dma((2, C, 4, 2)),
             dma((2, C, 4, 2)),
-            dma((2, C, 4, 2)),
-            dma((2, C, 4, 2)),
+            dma((2, R, 4, 2)),
+            dma((2, R, 4, 2)),
             dma((2, C)),
             dma((2, C)),
             dma((2, 2, C)),
             dma((2, 2, C)),
             dma((2, 2, C)),
             dma((2, 2, C)),
-            dma((2, C)),
-            dma((2, C)),
+            dma((2, R)),
+            dma((2, R)),
             dma((2, C)),
         ],
         compiler_params=pltpu.CompilerParams(
@@ -537,7 +550,7 @@
         cost_estimate=pl.CostEstimate(
             flops=24 * 10**9, bytes_accessed=8 * 2**20, transcendentals=4 * 2**20
         ),
-    )(kept, tokens, out_cot, w_in.reshape(C * NB * 8, BLK), w_out.reshape(C * NB * 8, BLK))
+    )(kept.T, tokens, out_cot, w_in.reshape(C * NB * 8, BLK), w_out.reshape(C * NB * 8, BLK))
     mixed, tokens_grad, w_in_grad, w_out_grad = pl.pallas_call(
         hand_over,
         out_shape=tuple(jax.ShapeDtypeStruct(r.shape, r.dtype) for r in results),

time: 162 us -> 160 us (0.988)
  no operation moved by 1% of the time
where the time goes in v3:
time: 160 us
  Pallas kernels  159 us (99%)
    pallas_call x1, Pallas kernels, per_device(): pl.pallas_call(kernel, out_shape=(jax.ShapeDtypeStruct(tokens.shape, BF16...  156 us

profile of v3, /device:TPU:0, one launch (start us, length us, event | category | flops | bytes accessed | tf_op | source)
XLA Modules:
  0.0 159.6 jit_solution(2282144988280305056)
XLA Ops:
  0.6 156.2 %shard_map.84 = (bf16[512,1024]{1,0:T(8,128)(2,1)}, bf16[512,1024]{1,0:T(8,128)(2,1)}, f32[8,6,8,256]{3,2,1,0:T(8,128)}, f32[8,6,8,256]{3,2,1,0:T(8,128)}) custom-call(s32[2,16]{1,0:T(2,128)} %bitcast.9, bf16[512,1024]{1,0:T(8,128)(2,1)} %tokens.1, bf16[512,1024]{1,0:T(8,128)(2,1)} %out_cot.1, bf16[384,256]{1,0:T(8,128)(2,1)} %bitcast.7, ...), custom_call_target="tpu_custom_call" | custom-call | flops 24000000000 | bytes 8388608 | tf_op jit(solution)/shard_map/pallas_call | solution.py:499
  156.8 2.8 %shard_map.85 = (bf16[512,1024]{1,0:T(8,128)(2,1)}, bf16[512,1024]{1,0:T(8,128)(2,1)}, f32[8,6,8,256]{3,2,1,0:T(8,128)}, f32[8,6,8,256]{3,2,1,0:T(8,128)}) custom-call(bf16[512,1024]{1,0:T(8,128)(2,1)} %get-tuple-element.12.refs_0_, bf16[512,1024]{1,0:T(8,128)(2,1)} %get-tuple-element.13.refs_1_, f32[8,6,8,256]{3,2,1,0:T(8,128)} %get-tuple-element.14.refs_2_, ...), custom_call_target="tpu_custom_call" | custom-call | tf_op jit(solution)/shard_map/pallas_call | solution.py:554

commit v4 on v3

--- a/solution.py
+++ b/solution.py
@@ -455,11 +455,12 @@
         event(u, 4, rs_three, R)
         event(u, 5, rs_four, R)
 
-        @pl.when(u == R + 2)
+        event(u, 3, rs_two, R)
+
+        @pl.when(u == R + 1)
         def _():
             finish()
 
-        event(u, 3, rs_two, R)
         event(u, 6, rs_last, R)
         event(u, 6, scatter_sent, R)
         event(u, 4, gather_sent)

time: 160 us -> 158 us (0.988)
  no operation moved by 1% of the time
where the time goes in v4:
time: 158 us
  Pallas kernels  158 us (100%)
    pallas_call x1, Pallas kernels, per_device(): pl.pallas_call(kernel, out_shape=(jax.ShapeDtypeStruct(tokens.shape, BF16...  155 us

profile of v4, /device:TPU:0, one launch (start us, length us, event | category | flops | bytes accessed | tf_op | source)
XLA Modules:
  0.0 158.2 jit_solution(11869507237446776273)
XLA Ops:
  0.6 154.7 %shard_map.84 = (bf16[512,1024]{1,0:T(8,128)(2,1)}, bf16[512,1024]{1,0:T(8,128)(2,1)}, f32[8,6,8,256]{3,2,1,0:T(8,128)}, f32[8,6,8,256]{3,2,1,0:T(8,128)}) custom-call(s32[2,16]{1,0:T(2,128)} %bitcast.9, bf16[512,1024]{1,0:T(8,128)(2,1)} %tokens.1, bf16[512,1024]{1,0:T(8,128)(2,1)} %out_cot.1, bf16[384,256]{1,0:T(8,128)(2,1)} %bitcast.7, ...), custom_call_target="tpu_custom_call" | custom-call | flops 24000000000 | bytes 8388608 | tf_op jit(solution)/shard_map/pallas_call | solution.py:500
  155.4 2.8 %shard_map.85 = (bf16[512,1024]{1,0:T(8,128)(2,1)}, bf16[512,1024]{1,0:T(8,128)(2,1)}, f32[8,6,8,256]{3,2,1,0:T(8,128)}, f32[8,6,8,256]{3,2,1,0:T(8,128)}) custom-call(bf16[512,1024]{1,0:T(8,128)(2,1)} %get-tuple-element.12.refs_0_, bf16[512,1024]{1,0:T(8,128)(2,1)} %get-tuple-element.13.refs_1_, f32[8,6,8,256]{3,2,1,0:T(8,128)} %get-tuple-element.14.refs_2_, ...), custom_call_target="tpu_custom_call" | custom-call | tf_op jit(solution)/shard_map/pallas_call | solution.py:555

commit v5 on v4

--- a/solution.py
+++ b/solution.py
@@ -452,10 +452,10 @@
         event(u, 0, rs_start, R)
         event(u, 2, rs_one, R)
         event(u, 0, compute_two, R)
+        event(u, 3, rs_two, R)
         event(u, 4, rs_three, R)
         event(u, 5, rs_four, R)
 
-        event(u, 3, rs_two, R)
 
         @pl.when(u == R + 1)
         def _():

time: 158 us -> 157 us (level)
  no operation moved by 1% of the time
where the time goes in v5:
time: 157 us
  Pallas kernels  157 us (100%)
    pallas_call x1, Pallas kernels, per_device(): pl.pallas_call(kernel, out_shape=(jax.ShapeDtypeStruct(tokens.shape, BF16...  154 us

profile of v5, /device:TPU:0, one launch (start us, length us, event | category | flops | bytes accessed | tf_op | source)
XLA Modules:
  0.0 157.3 jit_solution(4450885787071243605)
XLA Ops:
  0.6 153.9 %shard_map.84 = (bf16[512,1024]{1,0:T(8,128)(2,1)}, bf16[512,1024]{1,0:T(8,128)(2,1)}, f32[8,6,8,256]{3,2,1,0:T(8,128)}, f32[8,6,8,256]{3,2,1,0:T(8,128)}) custom-call(s32[2,16]{1,0:T(2,128)} %bitcast.9, bf16[512,1024]{1,0:T(8,128)(2,1)} %tokens.1, bf16[512,1024]{1,0:T(8,128)(2,1)} %out_cot.1, bf16[384,256]{1,0:T(8,128)(2,1)} %bitcast.7, ...), custom_call_target="tpu_custom_call" | custom-call | flops 24000000000 | bytes 8388608 | tf_op jit(solution)/shard_map/pallas_call | solution.py:500
  154.5 2.8 %shard_map.85 = (bf16[512,1024]{1,0:T(8,128)(2,1)}, bf16[512,1024]{1,0:T(8,128)(2,1)}, f32[8,6,8,256]{3,2,1,0:T(8,128)}, f32[8,6,8,256]{3,2,1,0:T(8,128)}) custom-call(bf16[512,1024]{1,0:T(8,128)(2,1)} %get-tuple-element.12.refs_0_, bf16[512,1024]{1,0:T(8,128)(2,1)} %get-tuple-element.13.refs_1_, f32[8,6,8,256]{3,2,1,0:T(8,128)} %get-tuple-element.14.refs_2_, ...), custom_call_target="tpu_custom_call" | custom-call | tf_op jit(solution)/shard_map/pallas_call | solution.py:555
